TPU v7x, 32 devices: a whole 2x2x4 slice. The times are simulated.
32 devices in a mesh: gx: 8 (over y, x, core), gy: 4 (over z).
Axes of the slice: x: 2, y: 2, z: 4, core: 2. Of those that a mesh axis runs over, the one named last changes fastest.
Arguments:
- src_coef: bfloat16 [512, 16384], P(None, ('gx', 'gy')), may hold values from -6 to 6
- point_slot: int32 [1024, 1024], P(None, ('gx', 'gy')), may hold values from 0 to 3
- tgt_owner: int32 [1024, 4], P(('gx', 'gy')), may hold values from 0 to 31, all different within a row; in each aligned block of 32 rows (0 to 31, 32 to 63, ...) at most 8 rows name the same one
- tgt_local: int32 [1024, 4], P(('gx', 'gy')), may hold values from 0 to 31
- vander: bfloat16 [1024, 512], replicated, may hold values from -0.25 to 0.25
- test_fn: bfloat16 [1024, 512], replicated, may hold values from -0.375 to 0.375
- inv_mass: float32 [512, 512], replicated, may hold values from -0.02 to 0.8, as said below
- jacobian: float32 [1024], P(('gx', 'gy')), may hold values from 0.5 to 2
- trace_tab: float32 [512, 128], replicated, may hold values from -0.25 to 0.25
- lift_tab: float32 [128, 512], replicated, may hold values from -0.5 to 0.5
- wave_speed: float32 [16], replicated, may hold values from 0.1 to 0.5
Outputs:
- remapped: float32 [1024, 16, 512], P(('gx', 'gy'))
Inputs may be any that keep to these rules, and one draw needn't show every extreme that they name: `tgt_owner`: each source element's 4 intersections have 4 different owners; among the source elements of one device at most 8 intersections have the same owner, and that many in every draw. `inv_mass`: symmetric positive definite.
All inputs are finite; a program needn't handle non-finite values.
Results may differ from a plain program's by a relative error of at most 0.0041.
Values may be sent and summed in bfloat16 or wider, within the bound.
A program may use at most 64 MiB of HBM per device.

v0:
```python
import functools

import jax
import jax.numpy as jnp
from jax import lax
from jax.experimental import pallas as pl
from jax.experimental.pallas import tpu as pltpu
from jax.sharding import Mesh, PartitionSpec as P

TX = 8
MESH = pl.DeviceIdType.MESH
GROUP = ("hi", "lo")
WORLD = ("hi", "rep", "lo")


def dot(a, b, dims, precision=None):
    return lax.dot_general(
        a, b, (dims, ((), ())), precision=precision, preferred_element_type=jnp.float32
    )


def neighbour_traces(traces, gx, gy, tx, ty):
    face_cols = traces.shape[1]
    pts = face_cols // 4
    grid = traces.reshape(gx, gy, tx, ty, face_cols).transpose(0, 2, 1, 3, 4)
    grid = grid.reshape(gx * tx, gy * ty, face_cols)
    face = lambda k: grid[:, :, k * pts : (k + 1) * pts]
    west = jnp.pad(face(1)[:-1], ((1, 0), (0, 0), (0, 0)))
    east = jnp.pad(face(0)[1:], ((0, 1), (0, 0), (0, 0)))
    south = jnp.pad(face(3)[:, :-1], ((0, 0), (1, 0), (0, 0)))
    north = jnp.pad(face(2)[:, 1:], ((0, 0), (0, 1), (0, 0)))
    joined = jnp.concatenate([west, east, south, north], axis=2) - grid
    joined = joined.reshape(gx, tx, gy, ty, face_cols).transpose(0, 2, 1, 3, 4)
    return joined.reshape(gx * gy * tx * ty, face_cols)


def peer_at(sizes, offset):
    return tuple(
        lax.rem(lax.axis_index(name) + step, size) if step else lax.axis_index(name)
        for name, size, step in zip(WORLD, sizes, offset)
    )


def offsets(sizes):
    hi, rep, lo = sizes
    every = [(a, b, c) for a in range(hi) for b in range(rep) for c in range(lo)]
    return every[1:]


def greet(peers):
    barrier = pltpu.get_barrier_semaphore()
    for peer in peers:
        pl.semaphore_signal(barrier, inc=1, device_id=peer, device_id_type=MESH)
    pl.semaphore_wait(barrier, len(peers))


def push(src, dst, send, recv, peer):
    copy = pltpu.make_async_remote_copy(
        src_ref=src, dst_ref=dst, send_sem=send, recv_sem=recv, device_id=peer, device_id_type=MESH
    )
    copy.start()
    return copy


def enter_kernel(
    sizes,
    blocks,
    slot_rows,
    meta,
    vander,
    test_fn,
    part,
    metas,
    mine,
    slots,
    onehot,
    pieces,
    block_sems,
    slot_sems,
    relay_sems,
    meta_sems,
    local_sems,
):
    hi, rep, lo = sizes
    h, r, l = (lax.axis_index(name) for name in WORLD)
    me = h * lo + l
    device = (h * rep + r) * lo + l
    everyone = offsets(sizes)
    group = [o for o in everyone if o[1] == 0]
    local = [
        pltpu.make_async_copy(slot_rows, slots.at[me], local_sems.at[0]),
        pltpu.make_async_copy(blocks.at[me], mine.at[me], local_sems.at[1]),
        pltpu.make_async_copy(meta, metas.at[device], local_sems.at[2]),
    ]
    for copy in local:
        copy.start()
    greet([peer_at(sizes, o) for o in everyone])

    along, relays = [], []
    for c in range(1, lo):
        peer = peer_at(sizes, (0, 0, c))
        along.append(
            push(slot_rows, slots.at[me], slot_sems.at[0, c], slot_sems.at[1, c], peer)
        )
    for a in range(1, hi):
        peer = peer_at(sizes, (a, 0, 0))
        k = a * lo
        relays.append(
            push(slot_rows, slots.at[me], relay_sems.at[0, k], relay_sems.at[1, k], peer)
        )
    arrive, labels = [], []
    for k, o in enumerate(group):
        to_h, _, to_l = peer = peer_at(sizes, o)
        arrive.append(
            push(
                blocks.at[to_h * lo + to_l],
                mine.at[me],
                block_sems.at[0, k],
                block_sems.at[1, k],
                peer,
            )
        )
    for k, o in enumerate(everyone):
        labels.append(
            push(
                meta, metas.at[device], meta_sems.at[0, k], meta_sems.at[1, k], peer_at(sizes, o)
            )
        )
    for c in range(1, lo):
        along[c - 1].wait_recv()
        place = h * lo + lax.rem(l + lo - c, lo)
        for a in range(1, hi):
            k = a * lo + c
            relays.append(
                push(
                    slots.at[place],
                    slots.at[place],
                    relay_sems.at[0, k],
                    relay_sems.at[1, k],
                    peer_at(sizes, (a, 0, 0)),
                )
            )
    for copy in local:
        copy.wait()
    for copy in labels:
        copy.wait_recv()

    width = meta.shape[1]
    rows = 128

    @pl.loop(0, part.shape[0] // rows)
    def _(i):
        start = pl.multiple_of(i * rows, rows)
        target = (lax.broadcasted_iota(jnp.int32, (rows, width), 0) + start).astype(jnp.float32)
        for g in range(hi * lo):
            ids = metas[(g // lo * rep + r) * lo + g % lo][0:1, :]
            onehot[pl.ds(start, rows), g * width : (g + 1) * width] = jnp.where(
                target == ids, 1.0, 0.0
            ).astype(onehot.dtype)

    members = slot_rows.shape[0]
    slot_count = width // members
    for a in range(hi):
        for c in range(lo):
            if a or c:
                arrive[a * lo + c - 1].wait_recv()
            if a:
                relays[(a - 1) if c == 0 else (hi - 1) * c + a - 1].wait_recv()
        from_h = lax.rem(h + hi - a, hi)
        first = from_h * lo
        source = mine[pl.ds(first, lo)].reshape(lo * members, -1)
        values = dot(source, vander[...], ((1,), (1,)))
        parts = []
        for c in range(lo):
            where = slots[first + c].astype(jnp.float32)
            value = values[c * members : (c + 1) * members]
            for s in range(slot_count):
                parts.append(jnp.where(where == s, value, 0.0).astype(jnp.bfloat16))
        masked = jnp.concatenate(parts, axis=0)
        pieces[from_h] = dot(masked, test_fn[...], ((1,), (0,))).astype(jnp.bfloat16)

    every = pieces.shape[0] * pieces.shape[1]
    block = 256

    @pl.loop(0, part.shape[0] // block)
    def _(i):
        start = pl.multiple_of(i * block, block)
        summed = dot(
            onehot[pl.ds(start, block), :], pieces[...].reshape(every, -1), ((1,), (0,))
        )
        part[pl.ds(start, block), :] = summed.astype(part.dtype)

    for copy in along + relays + arrive + labels:
        copy.wait_send()


def enter(sizes, blocks, slot_rows, meta, vander, test_fn):
    hi, rep, lo = sizes
    world = hi * rep * lo
    _, members, modes = blocks.shape
    vmem = pl.BlockSpec(memory_space=pltpu.VMEM)
    dma = pltpu.SemaphoreType.DMA
    return pl.pallas_call(
        functools.partial(enter_kernel, sizes),
        out_shape=(
            jax.ShapeDtypeStruct((world * members, modes), jnp.bfloat16),
            jax.ShapeDtypeStruct((world, *meta.shape), meta.dtype),
        ),
        in_specs=[vmem] * 5,
        out_specs=(vmem,) * 2,
        scratch_shapes=[
            pltpu.VMEM(blocks.shape, blocks.dtype),
            pltpu.VMEM((hi * lo, *slot_rows.shape), slot_rows.dtype),
            pltpu.VMEM((world * members, hi * lo * meta.shape[1]), jnp.bfloat16),
            pltpu.VMEM((hi, lo * meta.shape[1], modes), jnp.bfloat16),
            dma((2, hi * lo)),
            dma((2, lo)),
            dma((2, hi * lo)),
            dma((2, world)),
            dma((3,)),
        ],
        compiler_params=pltpu.CompilerParams(
            collective_id=0, has_side_effects=True, vmem_limit_bytes=44 << 20
        ),
        name="enter",
    )(blocks, slot_rows, meta, vander, test_fn)


def leave_kernel(sizes, blocks, mine, sems, local_sem):
    hi, rep, lo = sizes
    me = lax.axis_index("hi") * lo + lax.axis_index("lo")
    group = [o for o in offsets(sizes) if o[1] == 0]
    local = pltpu.make_async_copy(blocks.at[me], mine.at[me], local_sem)
    local.start()
    greet([peer_at(sizes, o) for o in group])
    copies = []
    for k, o in enumerate(group):
        to_h, _, to_l = peer = peer_at(sizes, o)
        copies.append(
            push(blocks.at[to_h * lo + to_l], mine.at[me], sems.at[0, k], sems.at[1, k], peer)
        )
    for copy in copies:
        copy.wait()
    local.wait()


def leave(sizes, blocks):
    vmem = pl.BlockSpec(memory_space=pltpu.VMEM)
    dma = pltpu.SemaphoreType.DMA
    return pl.pallas_call(
        functools.partial(leave_kernel, sizes),
        out_shape=jax.ShapeDtypeStruct(blocks.shape, blocks.dtype),
        in_specs=[vmem],
        out_specs=vmem,
        scratch_shapes=[dma((2, sizes[0] * sizes[2])), dma],
        compiler_params=pltpu.CompilerParams(
            collective_id=1, has_side_effects=True, vmem_limit_bytes=8 << 20
        ),
        name="leave",
    )(blocks)


def per_device(
    gx,
    gy,
    src_coef,
    point_slot,
    tgt_owner,
    tgt_local,
    vander,
    test_fn,
    inv_mass,
    jacobian,
    trace_tab,
    lift_tab,
    wave_speed,
):
    bf16 = jnp.bfloat16
    high = lax.Precision.HIGH
    modes, columns = src_coef.shape
    members = point_slot.shape[1]
    fields = wave_speed.shape[0]
    reps = lax.axis_size("rep")
    my_rep = lax.axis_index("rep")
    my_field = lax.axis_index("hi") * lax.axis_size("lo") + lax.axis_index("lo")

    row = jnp.arange(columns, dtype=jnp.int32)
    wanted = (row % members) * fields + row // members
    perm = (wanted[:, None] == row[None, :]).astype(bf16)
    by_field = dot(perm, src_coef, ((1,), (1,))).astype(bf16)
    sizes = tuple(lax.axis_size(name) for name in WORLD)
    holders = sizes[0] * sizes[2]
    ids = (tgt_owner * members + tgt_local).T.reshape(1, -1).astype(jnp.float32)
    jac = jnp.pad(jacobian[None, :], ((0, 0), (0, ids.shape[1] - members)))
    meta = jnp.pad(jnp.concatenate([ids, jac], axis=0), ((0, 6), (0, 0)))
    part, metas = enter(
        sizes,
        by_field.reshape(holders, members, modes),
        point_slot.T.astype(bf16),
        meta,
        vander,
        test_fn,
    )
    jac = metas[:, 1, :members].reshape(-1, 1)
    if reps == 2:
        other = lax.ppermute(part, "rep", [(0, 1), (1, 0)])
        moments = part.astype(jnp.float32) + other.astype(jnp.float32)
    else:
        moments = lax.psum(part.astype(jnp.float32), "rep")

    coeffs = dot(moments, inv_mass, ((1,), (0,)), high) / jac
    traces = dot(coeffs, trace_tab, ((1,), (0,)), high)
    jumps = neighbour_traces(traces, gx, gy, TX, members // TX)
    own = lambda x: lax.dynamic_index_in_dim(
        x.reshape(-1, reps, gy * members, x.shape[-1]), my_rep, 1, keepdims=False
    ).reshape(-1, x.shape[-1])
    lift = dot(lift_tab, inv_mass, ((1,), (0,)), high)
    speed = lax.dynamic_index_in_dim(wave_speed, my_field, 0, keepdims=False)
    update = dot(own(jumps), lift, ((1,), (0,)), high) * (speed / own(jac))
    result = (own(coeffs) + update).astype(bf16)
    back = leave(sizes, result.reshape(holders, members, modes))
    back = back.transpose(1, 0, 2)
    return back.astype(jnp.float32)


def nt(a, b):
    return dot(a, b, ((1,), (1,)))


def nn(a, b):
    return dot(a, b, ((1,), (0,)))


def split(x):
    high = x.astype(jnp.bfloat16)
    return high, (x - high.astype(jnp.float32)).astype(jnp.bfloat16)


def nn3(a, b):
    (ah, al), (bh, bl) = split(a), split(b)
    return nn(ah, bh) + nn(al, bh) + nn(ah, bl)


def fused_kernel(
    sizes,
    gy,
    src,
    slot_rows,
    owner,
    local_id,
    jac,
    vander_hbm,
    test_hbm,
    inv_hbm,
    trace_hbm,
    lift_hbm,
    speeds,
    out,
    coef,
    slot_in,
    vander,
    test_fn,
    inv,
    trace,
    lift,
    inv_hi,
    inv_lo,
    table,
    lift_inv,
    blocks,
    mine,
    slots,
    meta,
    metas,
    onehot,
    acc,
    part,
    part_in,
    edge,
    edge_in,
    beside,
    result,
    back,
    load_sems,
    slot_send,
    slot_recv,
    block_send,
    block_recv,
    meta_send,
    meta_recv,
    core_send,
    core_recv,
    back_send,
    back_recv,
):
    hi, rep, lo = sizes
    bf16, f32 = jnp.bfloat16, jnp.float32
    h, r, l = (lax.axis_index(name) for name in WORLD)
    me = h * lo + l
    group = hi * lo
    members, points = slot_rows.shape
    modes, columns = src.shape
    slot_count = owner.shape[0]
    fields = columns // members
    ty = members // TX
    width = slot_count * members
    strip = gy * members
    half = hi * strip
    unit = lo * width

    loads = []
    for k, (a, b) in enumerate(
        [
            (src, coef),
            (slot_rows, slot_in),
            (vander_hbm, vander),
            (test_hbm, test_fn),
            (inv_hbm, inv),
            (trace_hbm, trace),
            (lift_hbm, lift),
        ]
    ):
        copy = pltpu.make_async_copy(a, b, load_sems.at[k])
        copy.start()
        loads.append(copy)

    y, x = h // 2, h % 2
    flip_x = y * 2 + (1 - x)
    flip_y = (1 - y) * 2 + x
    flip_xy = (1 - y) * 2 + (1 - x)
    near = [h, flip_x, flip_y, flip_xy]
    core = (h, 1 - r, l)

    barrier = pltpu.get_barrier_semaphore()
    for o in offsets((hi, 1, lo)):
        pl.semaphore_signal(
            barrier, inc=1, device_id=peer_at((hi, 1, lo), o), device_id_type=MESH
        )
    pl.semaphore_signal(barrier, inc=1, device_id=core, device_id_type=MESH)

    meta[...] = jnp.zeros_like(meta)
    meta[0:slot_count, 0:members] = (owner[...] * members + local_id[...]).astype(f32)
    meta[slot_count : slot_count + 1, 0:members] = jac[...]
    packed = meta[...]
    row = lax.broadcasted_iota(jnp.int32, packed.shape, 0)
    lane = lax.broadcasted_iota(jnp.int32, packed.shape, 1)
    ids = jnp.zeros_like(packed)
    for s in range(slot_count):
        turned = pltpu.roll(packed, s * members, 1) if s else packed
        ids = jnp.where((row == s) & (lane // members == s), turned, ids)
    ids = jnp.sum(ids, axis=0, keepdims=True)
    jacs = jnp.zeros_like(packed)
    for c in range(lo):
        turned = pltpu.roll(packed, c * members, 1) if c else packed
        here = (row == slot_count) & (lane // members == c) & (lane // members == l)
        jacs = jnp.where(here, turned, jacs)
    jacs = jnp.sum(jacs, axis=0, keepdims=True)
    packed = jnp.where(row == 0, ids, jnp.where(row == 1, jacs, 0.0))
    meta[...] = packed
    metas[me] = packed

    loads[1].wait()
    slots[me] = slot_in[...].astype(f32).astype(bf16)
    loads[0].wait()
    rows = lo * members
    r_iota = lax.broadcasted_iota(jnp.int32, (rows, columns), 0)
    c_iota = lax.broadcasted_iota(jnp.int32, (rows, columns), 1)
    for k in range(hi):
        wanted = (r_iota % members) * fields + r_iota // members + k * lo
        perm = (wanted == c_iota).astype(f32).astype(bf16)
        moved = nt(perm, coef[...]).astype(bf16)
        blocks[k * lo : (k + 1) * lo] = moved.reshape(lo, members, modes)
    mine[me] = blocks[me]

    pl.semaphore_wait(barrier, group)

    sent = []

    def slot_copy(at, k, to):
        return pltpu.make_async_remote_copy(
            src_ref=slots.at[at],
            dst_ref=slots.at[at],
            send_sem=slot_send.at[k],
            recv_sem=slot_recv.at[at],
            device_id=to,
            device_id_type=MESH,
        )

    def send_slot(at, to, when=None):
        copy = slot_copy(at, len(sent), to)
        sent.append((copy, when))
        if when is None:
            copy.start()
        else:
            pl.when(when)(copy.start)

    def wait_slot(at):
        slot_copy(at, 0, core).wait_recv()

    up, down = jnp.minimum(l + 1, lo - 1), jnp.maximum(l - 1, 0)
    send_slot(me, (h, r, up), l + 1 < lo)
    send_slot(me, (h, r, down), l > 0)
    send_slot(me, (flip_x, r, l))
    send_slot(me, (flip_y, r, l))

    others = []
    for k, to_h in enumerate(near):
        for c in range(1 if k == 0 else 0, lo):
            to_l = (l + c) % lo
            copy = pltpu.make_async_remote_copy(
                src_ref=blocks.at[to_h * lo + to_l],
                dst_ref=mine.at[me],
                send_sem=block_send.at[k * lo + c],
                recv_sem=block_recv.at[me],
                device_id=(to_h, r, to_l),
                device_id_type=MESH,
            )
            copy.start()
            others.append(copy)
    for k, to_h in enumerate(near):
        for c in range(1 if k == 0 else 0, lo):
            to_l = (l + c) % lo
            copy = pltpu.make_async_remote_copy(
                src_ref=meta,
                dst_ref=metas.at[me],
                send_sem=meta_send.at[k * lo + c],
                recv_sem=meta_recv.at[me],
                device_id=(to_h, r, to_l),
                device_id_type=MESH,
            )
            copy.start()
            others.append(copy)

    def wait_block(at):
        pltpu.make_async_remote_copy(
            src_ref=mine.at[at],
            dst_ref=mine.at[at],
            send_sem=block_send.at[0],
            recv_sem=block_recv.at[at],
            device_id=core,
            device_id_type=MESH,
        ).wait_recv()
        pltpu.make_async_remote_copy(
            src_ref=metas.at[at],
            dst_ref=metas.at[at],
            send_sem=meta_send.at[0],
            recv_sem=meta_recv.at[at],
            device_id=core,
            device_id_type=MESH,
        ).wait_recv()

    for copy in loads[2:]:
        copy.wait()
    high, low = split(inv[...])
    inv_hi[...] = high
    inv_lo[...] = low
    traced = nn3(inv[...], trace[...])
    pts = trace.shape[1] // 4
    table[:, : 4 * pts] = traced.astype(bf16)
    face = lax.broadcasted_iota(jnp.int32, traced.shape, 1) // pts
    swapped = jnp.where(
        face % 2 == 0, pltpu.roll(traced, 3 * pts, 1), pltpu.roll(traced, pts, 1)
    )
    table[:, 4 * pts :] = swapped.astype(bf16)
    lift_inv[...] = nn3(lift[...], inv[...]).astype(bf16)

    def relay(z, ok, to, forward):
        z = jnp.clip(z, 0, lo - 1)

        @pl.when(ok)
        def _():
            wait_slot(h * lo + z)

        send_slot(h * lo + z, (h, r, to), ok & forward)
        send_slot(h * lo + z, (flip_x, r, l), ok)
        send_slot(h * lo + z, (flip_y, r, l), ok)

    def turn(z, ok):
        z = jnp.clip(z, 0, lo - 1)

        @pl.when(ok)
        def _():
            wait_slot(flip_x * lo + z)
            wait_slot(flip_y * lo + z)

        send_slot(flip_x * lo + z, (flip_y, r, l), ok & (z % 2 == 0))
        send_slot(flip_y * lo + z, (flip_x, r, l), ok & (z % 2 == 1))

    def relays(k):
        relay(l - k, l >= k, up, l + 1 < lo)
        relay(l + k, l + k < lo, down, l > 0)

    def turns(k):
        if k:
            turn(l - k, l >= k)
            turn(l + k, l + k < lo)
        else:
            turn(l, l >= 0)

    place = lax.broadcasted_iota(jnp.int32, (half, width), 0)
    place = (place // strip) * (2 * strip) + place % strip

    def gather(from_h, k):
        first = from_h * lo
        source = mine[pl.ds(first, lo)].reshape(lo * members, modes)
        values = nt(source, vander[...]).astype(bf16).astype(f32)
        parts = []
        for c in range(lo):
            where = slots[first + c].astype(f32)
            value = values[c * members : (c + 1) * members]
            for s in range(slot_count):
                parts.append(jnp.where(where == s, value, 0.0).astype(bf16))
        pieces = nn(jnp.concatenate(parts, axis=0), test_fn[...]).astype(bf16)
        for side in range(2):
            shift = (1 - r if side == 0 else r) * strip
            for c in range(lo):
                targets = (metas[first + c][0:1, :]).astype(jnp.int32) - shift
                onehot[side, :, c * width : (c + 1) * width] = (
                    jnp.where(place == targets, 1.0, 0.0).astype(bf16)
                )
        return pieces

    def scatter(pieces, side, first):
        summed = nn(onehot[side], pieces)
        return summed if first else acc[side] + summed

    for k in range(1, lo):
        relays(k)
        turns(k - 1)
    for k in range(hi):
        from_h = near[k]
        if k == 1:
            turns(lo - 1)
        if k == 3:
            for c in range(lo):
                wait_slot(from_h * lo + c)
        for c in range(1 if k == 0 else 0, lo):
            wait_block(from_h * lo + (l + c) % lo)
        pieces = gather(from_h, k)
        if k < hi - 1:
            for side in range(2):
                acc[side] = scatter(pieces, side, k == 0)

    def core_copy(a, b, k):
        return pltpu.make_async_remote_copy(
            src_ref=a,
            dst_ref=b,
            send_sem=core_send.at[k],
            recv_sem=core_recv.at[k],
            device_id=core,
            device_id_type=MESH,
        )

    theirs = scatter(pieces, 0, False).astype(bf16)
    part[...] = theirs
    part_copy = core_copy(part, part_in, 0)
    part_copy.start()
    ours = scatter(pieces, 1, False)
    acc[1] = ours
    swap = table[:, 4 * pts :]
    seen = nn(ours.astype(bf16), swap)
    eye_r = lax.broadcasted_iota(jnp.int32, (strip, strip), 0)
    eye_c = lax.broadcasted_iota(jnp.int32, (strip, strip), 1)
    lanes = lax.broadcasted_iota(jnp.int32, (strip, 4 * pts), 1)
    inverse = []
    for k in range(hi):
        jac_row = metas[k * lo][1:2, :]
        for c in range(1, lo):
            jac_row = jac_row + metas[k * lo + c][1:2, :]
        column = jnp.sum(jnp.where(eye_r == eye_c, jac_row, 0.0), axis=1, keepdims=True)
        column = 1.0 / column
        inverse.append(column)
        edge[k * strip : (k + 1) * strip, :] = jnp.where(
            lanes == 4 * pts - 1, column, seen[k * strip : (k + 1) * strip]
        )
    edge_copy = core_copy(edge, edge_in, 1)
    edge_copy.start()
    seen = nn(theirs, swap)
    beside[0:strip, :] = jnp.zeros((strip, 4 * pts), f32)
    beside[(hi + 1) * strip :, :] = jnp.zeros((strip, 4 * pts), f32)
    part_copy.wait_recv()
    edge_copy.wait_recv()
    for k in range(hi):
        got = edge_in[k * strip : (k + 1) * strip, :]
        column = got[:, 4 * pts - 1 : 4 * pts]
        beside[(k + 1) * strip : (k + 2) * strip, :] = (
            seen[k * strip : (k + 1) * strip] + got
        ) * column

    speed = speeds[me]
    t_row = lax.broadcasted_iota(jnp.int32, (strip, 4 * pts), 0)
    d_row, a_row, b_row = t_row // members, (t_row % members) // ty, t_row % ty
    face = lanes // pts
    moved = lambda v, n: pltpu.roll(v, n % strip, 0)
    for k in range(hi):
        own = slice(k * strip, (k + 1) * strip)
        moments = acc[1, own, :] + part_in[own, :].astype(f32)
        m_hi, m_lo = split(moments)
        both = nn(m_hi, table[...]) * inverse[k]
        mine_t, cur = both[:, : 4 * pts], both[:, 4 * pts :]
        prev = beside[pl.ds(pl.multiple_of((k + r) * strip, strip), strip), :]
        after = beside[pl.ds(pl.multiple_of((k + r + 1) * strip, strip), strip), :]
        last = (TX - 1) * ty
        west = jnp.where(a_row > 0, moved(cur, ty), moved(prev, -last))
        east = jnp.where(a_row < TX - 1, moved(cur, -ty), moved(after, last))
        jump = members - (ty - 1)
        south = jnp.where(b_row > 0, moved(cur, 1), moved(cur, jump))
        south = jnp.where((b_row == 0) & (d_row == 0), 0.0, south)
        north = jnp.where(b_row < ty - 1, moved(cur, -1), moved(cur, -jump))
        north = jnp.where((b_row == ty - 1) & (d_row == gy - 1), 0.0, north)
        other = jnp.where(
            face < 2, jnp.where(face == 0, west, east), jnp.where(face == 2, south, north)
        )
        jumps = ((other - mine_t) * speed).astype(bf16)
        solved = nn(m_hi, inv_hi[...]) + nn(m_lo, inv_hi[...]) + nn(m_hi, inv_lo[...])
        solved = (solved + nn(jumps, lift_inv[...])) * inverse[k]
        result[k * lo : (k + 1) * lo] = solved.astype(bf16).reshape(lo, members, modes)
        for c in range(lo):
            to_l = (l + c) % lo

            def back_copy():
                return pltpu.make_async_remote_copy(
                    src_ref=result.at[k * lo + to_l],
                    dst_ref=back.at[me],
                    send_sem=back_send.at[k * lo + c],
                    recv_sem=back_recv.at[me],
                    device_id=(k, r, to_l),
                    device_id_type=MESH,
                )

            if c == 0:
                pl.when(h != k)(lambda: back_copy().start())
            else:
                back_copy().start()
    back[me] = result[me]

    for at in range(group):

        @pl.when(me != at)
        def _():
            pltpu.make_async_remote_copy(
                src_ref=back.at[at],
                dst_ref=back.at[at],
                send_sem=back_send.at[0],
                recv_sem=back_recv.at[at],
                device_id=core,
                device_id_type=MESH,
            ).wait_recv()

    for at in range(group):
        out[:, at, :] = back[at].astype(f32)

    for copy, when in sent:
        if when is None:
            copy.wait_send()
        else:
            pl.when(when)(copy.wait_send)
    for copy in others + [part_copy, edge_copy]:
        copy.wait_send()
    for k in range(hi):
        for c in range(lo):

            def leave_wait():
                pltpu.make_async_remote_copy(
                    src_ref=result.at[k * lo],
                    dst_ref=back.at[me],
                    send_sem=back_send.at[k * lo + c],
                    recv_sem=back_recv.at[me],
                    device_id=core,
                    device_id_type=MESH,
                ).wait_send()

            if c == 0:
                pl.when(h != k)(leave_wait)
            else:
                leave_wait()


def fused(sizes, gy, *args):
    src, slot_rows, owner, _, _, vander, test_fn, inv, trace, lift, speeds = args
    hi, rep, lo = sizes
    members, points = slot_rows.shape
    modes, columns = src.shape
    slot_count = owner.shape[0]
    group = hi * lo
    strip = gy * members
    half = hi * strip
    faces = trace.shape[1]
    width = slot_count * members
    bf16, f32 = jnp.bfloat16, jnp.float32
    any_, vmem = pl.BlockSpec(memory_space=pl.ANY), pl.BlockSpec(memory_space=pltpu.VMEM)
    smem = pl.BlockSpec(memory_space=pltpu.SMEM)
    dma = pltpu.SemaphoreType.DMA
    like = lambda a: pltpu.VMEM(a.shape, a.dtype)
    slot_sends = 4 + (lo - 1) * 6 + 2 + (lo - 1) * 4
    return pl.pallas_call(
        functools.partial(fused_kernel, sizes, gy),
        out_shape=jax.ShapeDtypeStruct((members, columns // members, modes), f32),
        in_specs=[any_, any_, vmem, vmem, vmem, any_, any_, any_, any_, any_, smem],
        out_specs=vmem,
        scratch_shapes=[
            like(src),
            like(slot_rows),
            like(vander),
            like(test_fn),
            like(inv),
            like(trace),
            like(lift),
            pltpu.VMEM(inv.shape, bf16),
            pltpu.VMEM(inv.shape, bf16),
            pltpu.VMEM((modes, 2 * faces), bf16),
            pltpu.VMEM(lift.shape, bf16),
            pltpu.VMEM((group, members, modes), bf16),
            pltpu.VMEM((group, members, modes), bf16),
            pltpu.VMEM((group, members, points), bf16),
            pltpu.VMEM((8, width), f32),
            pltpu.VMEM((group, 8, width), f32),
            pltpu.VMEM((2, half, lo * width), bf16),
            pltpu.VMEM((2, half, modes), f32),
            pltpu.VMEM((half, modes), bf16),
            pltpu.VMEM((half, modes), bf16),
            pltpu.VMEM((half, faces), f32),
            pltpu.VMEM((half, faces), f32),
            pltpu.VMEM((half + 2 * strip, faces), f32),
            pltpu.VMEM((group, members, modes), bf16),
            pltpu.VMEM((group, members, modes), bf16),
            dma((7,)),
            dma((slot_sends,)),
            dma((group,)),
            dma((group,)),
            dma((group,)),
            dma((group,)),
            dma((group,)),
            dma((2,)),
            dma((2,)),
            dma((group,)),
            dma((group,)),
        ],
        compiler_params=pltpu.CompilerParams(
            collective_id=2, has_side_effects=True, vmem_limit_bytes=56 << 20
        ),
        name="remap",
    )(*args)


def fused_device(sizes, gy, src_coef, point_slot, tgt_owner, tgt_local, vander, test_fn, inv_mass, jacobian, trace_tab, lift_tab, wave_speed):
    return fused(
        sizes,
        gy,
        src_coef,
        point_slot.T,
        tgt_owner.T,
        tgt_local.T,
        jacobian[None, :],
        vander,
        test_fn,
        inv_mass,
        trace_tab,
        lift_tab,
        wave_speed,
    )


def solution(mesh):
    gx, gy = mesh.shape["gx"], mesh.shape["gy"]
    devices = gx * gy

    def call(*args):
        fields = args[-1].shape[0]
        sizes = (fields // gy, devices // fields, gy)
        body = functools.partial(per_device, gx, gy)
        if sizes[:2] == (4, 2):
            body = functools.partial(fused_device, sizes, gy)
        return jax.shard_map(
            body,
            mesh=Mesh(mesh.devices.reshape(sizes), WORLD),
            in_specs=(
                P(None, WORLD),
                P(None, WORLD),
                P(WORLD, None),
                P(WORLD, None),
                P(),
                P(),
                P(),
                P(WORLD),
                P(),
                P(),
                P(),
            ),
            out_specs=P(WORLD, None, None),
            check_vma=False,
        )(*args)

    return call
```

profile of v0, /device:TPU:7, one launch (start us, length us, event | category | flops | bytes accessed | tf_op | source)
XLA Modules:
  0.0 53.0 jit_solution(3148152910524054605)
XLA Ops:
  0.0 50.7 %remap.1 = f32[32,16,512]{2,1,0:T(8,128)} custom-call(bf16[512,512]{1,0:T(8,128)(2,1)} %src.1, s32[32,1024]{1,0:T(8,128)} %bitcast.4, s32[4,32]{1,0:T(4,128)} %bitcast.5, s32[4,32]{1,0:T(4,128)} %bitcast.6, f32[1,32]{1,0:T(1,128)} %bitcast.7, bf16[1024,512]{1,0:T(8,128)(2,1)} %vander_hbm.1, bf16[1024,512]{1,0:T(8,128)(2,1)} %test_hbm.1, f32[512,512]{1,0:T(8,128)} %inv_hbm.1, ...), custom_call_target="tpu_custom_call" | custom-call | tf_op jit(solution)/shard_map/remap/pallas_call | solution.py:796
  50.7 2.3 %copy.13 = f32[32,16,512]{2,1,0:T(8,128)} copy(f32[32,16,512]{2,1,0:T(8,128)} %remap.1) | data formatting | bytes 2097152
where the time goes:
time: 53.2 us; the launch traced here: 53 us
  Pallas kernels  50.7 us (95%)
  local copies, waits for them, and re-layouts  2.31 us (4%)
    pallas_call x1, Pallas kernels, fused(): pl.pallas_call(functools.partial(fused_kernel, sizes, gy), out_shape=jax....  50.7 us
    unnamed x1, local copies, waits for them, and re-layouts  2.31 us

commit v1 on v0

--- a/solution.py
+++ b/solution.py
@@ -486,37 +486,34 @@
             device_id_type=MESH,
         )
 
-    def send_slot(at, to, when=None):
+    def send_slot(at, to):
         copy = slot_copy(at, len(sent), to)
-        sent.append((copy, when))
-        if when is None:
-            copy.start()
-        else:
-            pl.when(when)(copy.start)
+        sent.append(copy)
+        copy.start()
 
     def wait_slot(at):
         slot_copy(at, 0, core).wait_recv()
 
-    up, down = jnp.minimum(l + 1, lo - 1), jnp.maximum(l - 1, 0)
-    send_slot(me, (h, r, up), l + 1 < lo)
-    send_slot(me, (h, r, down), l > 0)
-    send_slot(me, (flip_x, r, l))
-    send_slot(me, (flip_y, r, l))
+    for c in (2, 1, 3):
+        send_slot(me, (h, r, (l + c) % lo))
+    for to_h in (flip_x, flip_y, flip_xy):
+        send_slot(me, (to_h, r, l))
 
     others = []
-    for k, to_h in enumerate(near):
-        for c in range(1 if k == 0 else 0, lo):
-            to_l = (l + c) % lo
-            copy = pltpu.make_async_remote_copy(
-                src_ref=blocks.at[to_h * lo + to_l],
-                dst_ref=mine.at[me],
-                send_sem=block_send.at[k * lo + c],
-                recv_sem=block_recv.at[me],
-                device_id=(to_h, r, to_l),
-                device_id_type=MESH,
-            )
-            copy.start()
-            others.append(copy)
+
+    def send_block(k, c):
+        to_h, to_l = near[k], (l + c) % lo
+        copy = pltpu.make_async_remote_copy(
+            src_ref=blocks.at[to_h * lo + to_l],
+            dst_ref=mine.at[me],
+            send_sem=block_send.at[k * lo + c],
+            recv_sem=block_recv.at[me],
+            device_id=(to_h, r, to_l),
+            device_id_type=MESH,
+        )
+        copy.start()
+        others.append(copy)
+
     for k, to_h in enumerate(near):
         for c in range(1 if k == 0 else 0, lo):
             to_l = (l + c) % lo
@@ -530,6 +527,21 @@
             )
             copy.start()
             others.append(copy)
+
+    line = [h * lo + (l + c) % lo for c in (1, 3, 2)]
+    for i, at in enumerate(line):
+        wait_slot(at)
+        send_slot(at, (flip_x, r, l))
+        send_block(1, (1, 3, 2)[i])
+        send_block(0, (1, 3, 2)[i])
+        send_slot(at, (flip_y, r, l))
+        send_block(2, (1, 3, 2)[i])
+    send_block(1, 0)
+    send_block(2, 0)
+    for i, at in enumerate(line):
+        send_slot(at, (flip_xy, r, l))
+        send_block(3, (1, 3, 2, 0)[i])
+    send_block(3, 0)
 
     def wait_block(at):
         pltpu.make_async_remote_copy(
@@ -563,39 +575,6 @@
     )
     table[:, 4 * pts :] = swapped.astype(bf16)
     lift_inv[...] = nn3(lift[...], inv[...]).astype(bf16)
-
-    def relay(z, ok, to, forward):
-        z = jnp.clip(z, 0, lo - 1)
-
-        @pl.when(ok)
-        def _():
-            wait_slot(h * lo + z)
-
-        send_slot(h * lo + z, (h, r, to), ok & forward)
-        send_slot(h * lo + z, (flip_x, r, l), ok)
-        send_slot(h * lo + z, (flip_y, r, l), ok)
-
-    def turn(z, ok):
-        z = jnp.clip(z, 0, lo - 1)
-
-        @pl.when(ok)
-        def _():
-            wait_slot(flip_x * lo + z)
-            wait_slot(flip_y * lo + z)
-
-        send_slot(flip_x * lo + z, (flip_y, r, l), ok & (z % 2 == 0))
-        send_slot(flip_y * lo + z, (flip_x, r, l), ok & (z % 2 == 1))
-
-    def relays(k):
-        relay(l - k, l >= k, up, l + 1 < lo)
-        relay(l + k, l + k < lo, down, l > 0)
-
-    def turns(k):
-        if k:
-            turn(l - k, l >= k)
-            turn(l + k, l + k < lo)
-        else:
-            turn(l, l >= 0)
 
     place = lax.broadcasted_iota(jnp.int32, (half, width), 0)
     place = (place // strip) * (2 * strip) + place % strip
@@ -624,14 +603,9 @@
         summed = nn(onehot[side], pieces)
         return summed if first else acc[side] + summed
 
-    for k in range(1, lo):
-        relays(k)
-        turns(k - 1)
     for k in range(hi):
         from_h = near[k]
-        if k == 1:
-            turns(lo - 1)
-        if k == 3:
+        if k:
             for c in range(lo):
                 wait_slot(from_h * lo + c)
         for c in range(1 if k == 0 else 0, lo):
@@ -750,12 +724,7 @@
     for at in range(group):
         out[:, at, :] = back[at].astype(f32)
 
-    for copy, when in sent:
-        if when is None:
-            copy.wait_send()
-        else:
-            pl.when(when)(copy.wait_send)
-    for copy in others + [part_copy, edge_copy]:
+    for copy in sent + others + [part_copy, edge_copy]:
         copy.wait_send()
     for k in range(hi):
         for c in range(lo):
@@ -792,10 +761,10 @@
     smem = pl.BlockSpec(memory_space=pltpu.SMEM)
     dma = pltpu.SemaphoreType.DMA
     like = lambda a: pltpu.VMEM(a.shape, a.dtype)
-    slot_sends = 4 + (lo - 1) * 6 + 2 + (lo - 1) * 4
+    slot_sends = 6 + (lo - 1) * 3
     return pl.pallas_call(
         functools.partial(fused_kernel, sizes, gy),
-        out_shape=jax.ShapeDtypeStruct((members, columns // members, modes), f32),
+        out_shape=pltpu.VMEM((members, columns // members, modes), f32),
         in_specs=[any_, any_, vmem, vmem, vmem, any_, any_, any_, any_, any_, smem],
         out_specs=vmem,
         scratch_shapes=[
@@ -869,7 +838,7 @@
         fields = args[-1].shape[0]
         sizes = (fields // gy, devices // fields, gy)
         body = functools.partial(per_device, gx, gy)
-        if sizes[:2] == (4, 2):
+        if sizes == (4, 2, 4):
             body = functools.partial(fused_device, sizes, gy)
         return jax.shard_map(
             body,

time: 53.2 us -> 47.6 us (0.89)
  the two profiles are of different devices: /device:TPU:7 before, /device:TPU:31 now
where the time goes in v1:
time: 47.6 us; the launch traced here: 47.5 us
  Pallas kernels  46.5 us (98%)
  local copies, waits for them, and re-layouts  0.97 us (2%)
    pallas_call x1, Pallas kernels, fused(): pl.pallas_call(functools.partial(fused_kernel, sizes, gy), out_shape=pltp...  46.5 us
    unnamed x1, local copies, waits for them, and re-layouts  0.97 us

profile of v1, /device:TPU:31, one launch (start us, length us, event | category | flops | bytes accessed | tf_op | source)
XLA Modules:
  0.0 47.5 jit_solution(7897683062731892685)
XLA Ops:
  0.0 46.5 %remap.1 = f32[32,16,512]{2,1,0:T(8,128)S(1)} custom-call(bf16[512,512]{1,0:T(8,128)(2,1)} %src.1, s32[32,1024]{1,0:T(8,128)} %bitcast.4, s32[4,32]{1,0:T(4,128)} %bitcast.5, s32[4,32]{1,0:T(4,128)} %bitcast.6, f32[1,32]{1,0:T(1,128)} %bitcast.7, bf16[1024,512]{1,0:T(8,128)(2,1)} %vander_hbm.1, bf16[1024,512]{1,0:T(8,128)(2,1)} %test_hbm.1, ...), custom_call_target="tpu_custom_call" | custom-call | tf_op jit(solution)/shard_map/remap/pallas_call | solution.py:765
  46.5 1.0 %copy.13 = f32[32,16,512]{2,1,0:T(8,128)} copy(f32[32,16,512]{2,1,0:T(8,128)S(1)} %remap.1) | data formatting | bytes 2097152

commit v2 on v1

--- a/solution.py
+++ b/solution.py
@@ -406,7 +406,6 @@
     width = slot_count * members
     strip = gy * members
     half = hi * strip
-    unit = lo * width
 
     loads = []
     for k, (a, b) in enumerate(
@@ -494,9 +493,10 @@
     def wait_slot(at):
         slot_copy(at, 0, core).wait_recv()
 
-    for c in (2, 1, 3):
-        send_slot(me, (h, r, (l + c) % lo))
-    for to_h in (flip_x, flip_y, flip_xy):
+    turns = (1, 3, 2)
+    for c in turns:
+        send_slot(me, (h, r, (l - c + lo) % lo))
+    for to_h in near[1:]:
         send_slot(me, (to_h, r, l))
 
     others = []
@@ -528,20 +528,15 @@
             copy.start()
             others.append(copy)
 
-    line = [h * lo + (l + c) % lo for c in (1, 3, 2)]
-    for i, at in enumerate(line):
+    for k in range(1, hi):
+        send_block(k, 0)
+    for c in turns:
+        at = h * lo + (l + c) % lo
         wait_slot(at)
-        send_slot(at, (flip_x, r, l))
-        send_block(1, (1, 3, 2)[i])
-        send_block(0, (1, 3, 2)[i])
-        send_slot(at, (flip_y, r, l))
-        send_block(2, (1, 3, 2)[i])
-    send_block(1, 0)
-    send_block(2, 0)
-    for i, at in enumerate(line):
-        send_slot(at, (flip_xy, r, l))
-        send_block(3, (1, 3, 2, 0)[i])
-    send_block(3, 0)
+        for k in (3, 1, 2, 0):
+            if k:
+                send_slot(at, (near[k], r, l))
+            send_block(k, (lo - c) % lo)
 
     def wait_block(at):
         pltpu.make_async_remote_copy(
@@ -579,21 +574,20 @@
     place = lax.broadcasted_iota(jnp.int32, (half, width), 0)
     place = (place // strip) * (2 * strip) + place % strip
 
-    def gather(from_h, k):
-        first = from_h * lo
-        source = mine[pl.ds(first, lo)].reshape(lo * members, modes)
+    def gather(places):
+        source = jnp.concatenate([mine[at] for at in places], axis=0)
         values = nt(source, vander[...]).astype(bf16).astype(f32)
         parts = []
-        for c in range(lo):
-            where = slots[first + c].astype(f32)
+        for c, at in enumerate(places):
+            where = slots[at].astype(f32)
             value = values[c * members : (c + 1) * members]
             for s in range(slot_count):
                 parts.append(jnp.where(where == s, value, 0.0).astype(bf16))
         pieces = nn(jnp.concatenate(parts, axis=0), test_fn[...]).astype(bf16)
         for side in range(2):
             shift = (1 - r if side == 0 else r) * strip
-            for c in range(lo):
-                targets = (metas[first + c][0:1, :]).astype(jnp.int32) - shift
+            for c, at in enumerate(places):
+                targets = (metas[at][0:1, :]).astype(jnp.int32) - shift
                 onehot[side, :, c * width : (c + 1) * width] = (
                     jnp.where(place == targets, 1.0, 0.0).astype(bf16)
                 )
@@ -603,15 +597,14 @@
         summed = nn(onehot[side], pieces)
         return summed if first else acc[side] + summed
 
-    for k in range(hi):
-        from_h = near[k]
-        if k:
-            for c in range(lo):
-                wait_slot(from_h * lo + c)
-        for c in range(1 if k == 0 else 0, lo):
-            wait_block(from_h * lo + (l + c) % lo)
-        pieces = gather(from_h, k)
-        if k < hi - 1:
+    for k, c in enumerate((0,) + turns):
+        places = [at * lo + (l + c) % lo for at in near]
+        for at in places[1:]:
+            wait_slot(at)
+        for at in places[0 if c else 1 :]:
+            wait_block(at)
+        pieces = gather(places)
+        if k < lo - 1:
             for side in range(2):
                 acc[side] = scatter(pieces, side, k == 0)
 
@@ -784,7 +777,7 @@
             pltpu.VMEM((group, members, points), bf16),
             pltpu.VMEM((8, width), f32),
             pltpu.VMEM((group, 8, width), f32),
-            pltpu.VMEM((2, half, lo * width), bf16),
+            pltpu.VMEM((2, half, hi * width), bf16),
             pltpu.VMEM((2, half, modes), f32),
             pltpu.VMEM((half, modes), bf16),
             pltpu.VMEM((half, modes), bf16),

time: 47.6 us -> 44.7 us (0.939)
  the two profiles are of different devices: /device:TPU:31 before, /device:TPU:7 now
where the time goes in v2:
time: 44.7 us; the launch traced here: 44.5 us
  Pallas kernels  43.5 us (97%)
  local copies, waits for them, and re-layouts  0.97 us (2%)
    pallas_call x1, Pallas kernels, fused(): pl.pallas_call(functools.partial(fused_kernel, sizes, gy), out_shape=pltp...  43.5 us
    unnamed x1, local copies, waits for them, and re-layouts  0.97 us

profile of v2, /device:TPU:7, one launch (start us, length us, event | category | flops | bytes accessed | tf_op | source)
XLA Modules:
  0.0 44.5 jit_solution(8490326257050672683)
XLA Ops:
  0.0 43.5 %remap.1 = f32[32,16,512]{2,1,0:T(8,128)S(1)} custom-call(bf16[512,512]{1,0:T(8,128)(2,1)} %src.1, s32[32,1024]{1,0:T(8,128)} %bitcast.4, s32[4,32]{1,0:T(4,128)} %bitcast.5, s32[4,32]{1,0:T(4,128)} %bitcast.6, f32[1,32]{1,0:T(1,128)} %bitcast.7, bf16[1024,512]{1,0:T(8,128)(2,1)} %vander_hbm.1, bf16[1024,512]{1,0:T(8,128)(2,1)} %test_hbm.1, ...), custom_call_target="tpu_custom_call" | custom-call | tf_op jit(solution)/shard_map/remap/pallas_call | solution.py:758
  43.6 1.0 %copy.13 = f32[32,16,512]{2,1,0:T(8,128)} copy(f32[32,16,512]{2,1,0:T(8,128)S(1)} %remap.1) | data formatting | bytes 2097152

commit v3 on v2

--- a/solution.py
+++ b/solution.py
@@ -407,6 +407,20 @@
     strip = gy * members
     half = hi * strip
 
+    y, x = h // 2, h % 2
+    flip_x = y * 2 + (1 - x)
+    flip_y = (1 - y) * 2 + x
+    flip_xy = (1 - y) * 2 + (1 - x)
+    near = [h, flip_x, flip_y, flip_xy]
+    core = (h, 1 - r, l)
+
+    barrier = pltpu.get_barrier_semaphore()
+    for o in offsets((hi, 1, lo)):
+        pl.semaphore_signal(
+            barrier, inc=1, device_id=peer_at((hi, 1, lo), o), device_id_type=MESH
+        )
+    pl.semaphore_signal(barrier, inc=1, device_id=core, device_id_type=MESH)
+
     loads = []
     for k, (a, b) in enumerate(
         [
@@ -423,19 +437,57 @@
         copy.start()
         loads.append(copy)
 
-    y, x = h // 2, h % 2
-    flip_x = y * 2 + (1 - x)
-    flip_y = (1 - y) * 2 + x
-    flip_xy = (1 - y) * 2 + (1 - x)
-    near = [h, flip_x, flip_y, flip_xy]
-    core = (h, 1 - r, l)
-
-    barrier = pltpu.get_barrier_semaphore()
-    for o in offsets((hi, 1, lo)):
-        pl.semaphore_signal(
-            barrier, inc=1, device_id=peer_at((hi, 1, lo), o), device_id_type=MESH
-        )
-    pl.semaphore_signal(barrier, inc=1, device_id=core, device_id_type=MESH)
+    loads[1].wait()
+    slots[me] = slot_in[...].astype(f32).astype(bf16)
+    pl.semaphore_wait(barrier, group)
+
+    sent = []
+
+    def slot_copy(at, k, to):
+        return pltpu.make_async_remote_copy(
+            src_ref=slots.at[at],
+            dst_ref=slots.at[at],
+            send_sem=slot_send.at[k],
+            recv_sem=slot_recv.at[at],
+            device_id=to,
+            device_id_type=MESH,
+        )
+
+    def send_slot(at, to):
+        copy = slot_copy(at, len(sent), to)
+        sent.append((copy, None))
+        copy.start()
+
+    def wait_slot(at):
+        slot_copy(at, 0, core).wait_recv()
+
+    partner = l + 1 - 2 * (l % 2)
+    lower = l < 2
+    near_z = jnp.where(lower, 2, 1)
+    far_z = jnp.where(lower, 3, 0)
+    inner = (l == 1) | (l == 2)
+    outer = jnp.where(lower, 0, 3)
+    line = [l, partner, near_z, far_z]
+
+    send_slot(me, (h, r, near_z))
+    send_slot(me, (h, r, partner))
+    for to_h in near[1:]:
+        send_slot(me, (to_h, r, l))
+
+    others = []
+
+    def send_block(k, c):
+        to_h, to_l = near[k], line[c]
+        copy = pltpu.make_async_remote_copy(
+            src_ref=blocks.at[to_h * lo + to_l],
+            dst_ref=mine.at[me],
+            send_sem=block_send.at[k * lo + c],
+            recv_sem=block_recv.at[me],
+            device_id=(to_h, r, to_l),
+            device_id_type=MESH,
+        )
+        copy.start()
+        others.append(copy)
 
     meta[...] = jnp.zeros_like(meta)
     meta[0:slot_count, 0:members] = (owner[...] * members + local_id[...]).astype(f32)
@@ -458,62 +510,6 @@
     meta[...] = packed
     metas[me] = packed
 
-    loads[1].wait()
-    slots[me] = slot_in[...].astype(f32).astype(bf16)
-    loads[0].wait()
-    rows = lo * members
-    r_iota = lax.broadcasted_iota(jnp.int32, (rows, columns), 0)
-    c_iota = lax.broadcasted_iota(jnp.int32, (rows, columns), 1)
-    for k in range(hi):
-        wanted = (r_iota % members) * fields + r_iota // members + k * lo
-        perm = (wanted == c_iota).astype(f32).astype(bf16)
-        moved = nt(perm, coef[...]).astype(bf16)
-        blocks[k * lo : (k + 1) * lo] = moved.reshape(lo, members, modes)
-    mine[me] = blocks[me]
-
-    pl.semaphore_wait(barrier, group)
-
-    sent = []
-
-    def slot_copy(at, k, to):
-        return pltpu.make_async_remote_copy(
-            src_ref=slots.at[at],
-            dst_ref=slots.at[at],
-            send_sem=slot_send.at[k],
-            recv_sem=slot_recv.at[at],
-            device_id=to,
-            device_id_type=MESH,
-        )
-
-    def send_slot(at, to):
-        copy = slot_copy(at, len(sent), to)
-        sent.append(copy)
-        copy.start()
-
-    def wait_slot(at):
-        slot_copy(at, 0, core).wait_recv()
-
-    turns = (1, 3, 2)
-    for c in turns:
-        send_slot(me, (h, r, (l - c + lo) % lo))
-    for to_h in near[1:]:
-        send_slot(me, (to_h, r, l))
-
-    others = []
-
-    def send_block(k, c):
-        to_h, to_l = near[k], (l + c) % lo
-        copy = pltpu.make_async_remote_copy(
-            src_ref=blocks.at[to_h * lo + to_l],
-            dst_ref=mine.at[me],
-            send_sem=block_send.at[k * lo + c],
-            recv_sem=block_recv.at[me],
-            device_id=(to_h, r, to_l),
-            device_id_type=MESH,
-        )
-        copy.start()
-        others.append(copy)
-
     for k, to_h in enumerate(near):
         for c in range(1 if k == 0 else 0, lo):
             to_l = (l + c) % lo
@@ -528,15 +524,33 @@
             copy.start()
             others.append(copy)
 
-    for k in range(1, hi):
-        send_block(k, 0)
-    for c in turns:
-        at = h * lo + (l + c) % lo
+    loads[0].wait()
+    rows = lo * members
+    r_iota = lax.broadcasted_iota(jnp.int32, (rows, columns), 0)
+    c_iota = lax.broadcasted_iota(jnp.int32, (rows, columns), 1)
+    r_iota = (r_iota % members) * fields + r_iota // members
+    for k in (1, 2, 3, 0):
+        first = near[k] * lo
+        perm = (r_iota + first == c_iota).astype(f32).astype(bf16)
+        moved = nt(perm, coef[...]).astype(bf16)
+        blocks[pl.ds(first, lo)] = moved.reshape(lo, members, modes)
+        if k:
+            send_block(k, 0)
+    mine[me] = blocks[me]
+
+
+    for i in range(1, lo):
+        z = line[i]
+        at = h * lo + z
         wait_slot(at)
+        if i > 1:
+            copy = slot_copy(at, len(sent), (h, r, outer))
+            sent.append((copy, inner))
+            pl.when(inner)(copy.start)
         for k in (3, 1, 2, 0):
-            if k:
+            if k in (1, 2, 3):
                 send_slot(at, (near[k], r, l))
-            send_block(k, (lo - c) % lo)
+            send_block(k, i)
 
     def wait_block(at):
         pltpu.make_async_remote_copy(
@@ -597,11 +611,11 @@
         summed = nn(onehot[side], pieces)
         return summed if first else acc[side] + summed
 
-    for k, c in enumerate((0,) + turns):
-        places = [at * lo + (l + c) % lo for at in near]
+    for k, z in enumerate(line):
+        places = [at * lo + z for at in near]
         for at in places[1:]:
             wait_slot(at)
-        for at in places[0 if c else 1 :]:
+        for at in places[0 if k else 1 :]:
             wait_block(at)
         pieces = gather(places)
         if k < lo - 1:
@@ -717,7 +731,12 @@
     for at in range(group):
         out[:, at, :] = back[at].astype(f32)
 
-    for copy in sent + others + [part_copy, edge_copy]:
+    for copy, when in sent:
+        if when is None:
+            copy.wait_send()
+        else:
+            pl.when(when)(copy.wait_send)
+    for copy in others + [part_copy, edge_copy]:
         copy.wait_send()
     for k in range(hi):
         for c in range(lo):
@@ -754,7 +773,7 @@
     smem = pl.BlockSpec(memory_space=pltpu.SMEM)
     dma = pltpu.SemaphoreType.DMA
     like = lambda a: pltpu.VMEM(a.shape, a.dtype)
-    slot_sends = 6 + (lo - 1) * 3
+    slot_sends = 8 + lo * 5
     return pl.pallas_call(
         functools.partial(fused_kernel, sizes, gy),
         out_shape=pltpu.VMEM((members, columns // members, modes), f32),

time: 44.7 us -> 44.4 us (level)
  no operation moved by 1% of the time
where the time goes in v3:
time: 44.4 us; the launch traced here: 44.2 us
  Pallas kernels  43.3 us (98%)
  local copies, waits for them, and re-layouts  0.97 us (2%)
    pallas_call x1, Pallas kernels, fused(): pl.pallas_call(functools.partial(fused_kernel, sizes, gy), out_shape=pltp...  43.3 us
    unnamed x1, local copies, waits for them, and re-layouts  0.97 us

profile of v3, /device:TPU:7, one launch (start us, length us, event | category | flops | bytes accessed | tf_op | source)
XLA Modules:
  0.0 44.2 jit_solution(7897221856618477089)
XLA Ops:
  0.0 43.3 %remap.1 = f32[32,16,512]{2,1,0:T(8,128)S(1)} custom-call(bf16[512,512]{1,0:T(8,128)(2,1)} %src.1, s32[32,1024]{1,0:T(8,128)} %bitcast.4, s32[4,32]{1,0:T(4,128)} %bitcast.5, s32[4,32]{1,0:T(4,128)} %bitcast.6, f32[1,32]{1,0:T(1,128)} %bitcast.7, bf16[1024,512]{1,0:T(8,128)(2,1)} %vander_hbm.1, bf16[1024,512]{1,0:T(8,128)(2,1)} %test_hbm.1, ...), custom_call_target="tpu_custom_call" | custom-call | tf_op jit(solution)/shard_map/remap/pallas_call | solution.py:777
  43.3 1.0 %copy.13 = f32[32,16,512]{2,1,0:T(8,128)} copy(f32[32,16,512]{2,1,0:T(8,128)S(1)} %remap.1) | data formatting | bytes 2097152

commit v4 on v3

--- a/solution.py
+++ b/solution.py
@@ -715,6 +715,31 @@
                 back_copy().start()
     back[me] = result[me]
 
+    for copy, when in sent:
+        if when is None:
+            copy.wait_send()
+        else:
+            pl.when(when)(copy.wait_send)
+    for copy in others + [part_copy, edge_copy]:
+        copy.wait_send()
+    for k in range(hi):
+        for c in range(lo):
+
+            def leave_wait():
+                pltpu.make_async_remote_copy(
+                    src_ref=result.at[k * lo],
+                    dst_ref=back.at[me],
+                    send_sem=back_send.at[k * lo + c],
+                    recv_sem=back_recv.at[me],
+                    device_id=core,
+                    device_id_type=MESH,
+                ).wait_send()
+
+            if c == 0:
+                pl.when(h != k)(leave_wait)
+            else:
+                leave_wait()
+
     for at in range(group):
 
         @pl.when(me != at)
@@ -730,31 +755,6 @@
 
     for at in range(group):
         out[:, at, :] = back[at].astype(f32)
-
-    for copy, when in sent:
-        if when is None:
-            copy.wait_send()
-        else:
-            pl.when(when)(copy.wait_send)
-    for copy in others + [part_copy, edge_copy]:
-        copy.wait_send()
-    for k in range(hi):
-        for c in range(lo):
-
-            def leave_wait():
-                pltpu.make_async_remote_copy(
-                    src_ref=result.at[k * lo],
-                    dst_ref=back.at[me],
-                    send_sem=back_send.at[k * lo + c],
-                    recv_sem=back_recv.at[me],
-                    device_id=core,
-                    device_id_type=MESH,
-                ).wait_send()
-
-            if c == 0:
-                pl.when(h != k)(leave_wait)
-            else:
-                leave_wait()
 
 
 def fused(sizes, gy, *args):

time: 44.4 us -> 44.3 us (level)
  no operation moved by 1% of the time
where the time goes in v4:
time: 44.3 us; the launch traced here: 44.1 us
  Pallas kernels  43.2 us (98%)
  local copies, waits for them, and re-layouts  0.97 us (2%)
    pallas_call x1, Pallas kernels, fused(): pl.pallas_call(functools.partial(fused_kernel, sizes, gy), out_shape=pltp...  43.2 us
    unnamed x1, local copies, waits for them, and re-layouts  0.97 us

profile of v4, /device:TPU:7, one launch (start us, length us, event | category | flops | bytes accessed | tf_op | source)
XLA Modules:
  0.0 44.1 jit_solution(6325030597630863579)
XLA Ops:
  0.0 43.2 %remap.1 = f32[32,16,512]{2,1,0:T(8,128)S(1)} custom-call(bf16[512,512]{1,0:T(8,128)(2,1)} %src.1, s32[32,1024]{1,0:T(8,128)} %bitcast.4, s32[4,32]{1,0:T(4,128)} %bitcast.5, s32[4,32]{1,0:T(4,128)} %bitcast.6, f32[1,32]{1,0:T(1,128)} %bitcast.7, bf16[1024,512]{1,0:T(8,128)(2,1)} %vander_hbm.1, bf16[1024,512]{1,0:T(8,128)(2,1)} %test_hbm.1, ...), custom_call_target="tpu_custom_call" | custom-call | tf_op jit(solution)/shard_map/remap/pallas_call | solution.py:777
  43.2 1.0 %copy.13 = f32[32,16,512]{2,1,0:T(8,128)} copy(f32[32,16,512]{2,1,0:T(8,128)S(1)} %remap.1) | data formatting | bytes 2097152

commit v5 on v4

--- a/solution.py
+++ b/solution.py
@@ -539,18 +539,33 @@
     mine[me] = blocks[me]
 
 
-    for i in range(1, lo):
-        z = line[i]
-        at = h * lo + z
-        wait_slot(at)
-        if i > 1:
-            copy = slot_copy(at, len(sent), (h, r, outer))
-            sent.append((copy, inner))
-            pl.when(inner)(copy.start)
-        for k in (3, 1, 2, 0):
-            if k in (1, 2, 3):
-                send_slot(at, (near[k], r, l))
-            send_block(k, i)
+    for k in (0, 3, 1, 2):
+        send_block(k, 2)
+    for k in (0, 3, 1, 2):
+        send_block(k, 3)
+    at = h * lo + line[2]
+    wait_slot(at)
+    copy = slot_copy(at, len(sent), (h, r, outer))
+    sent.append((copy, inner))
+    pl.when(inner)(copy.start)
+    send_slot(at, (near[3], r, l))
+    send_slot(at, (near[1], r, l))
+    send_slot(at, (near[2], r, l))
+    at = h * lo + line[3]
+    wait_slot(at)
+    copy = slot_copy(at, len(sent), (h, r, outer))
+    sent.append((copy, inner))
+    pl.when(inner)(copy.start)
+    send_slot(at, (near[3], r, l))
+    send_slot(at, (near[1], r, l))
+    send_slot(at, (near[2], r, l))
+    at = h * lo + line[1]
+    wait_slot(at)
+    send_slot(at, (near[3], r, l))
+    send_slot(at, (near[1], r, l))
+    send_slot(at, (near[2], r, l))
+    for k in (0, 3, 1, 2):
+        send_block(k, 1)
 
     def wait_block(at):
         pltpu.make_async_remote_copy(
@@ -590,13 +605,13 @@
 
     def gather(places):
         source = jnp.concatenate([mine[at] for at in places], axis=0)
-        values = nt(source, vander[...]).astype(bf16).astype(f32)
+        values = nt(source, vander[...]).astype(bf16)
         parts = []
         for c, at in enumerate(places):
-            where = slots[at].astype(f32)
+            where = slots[at]
             value = values[c * members : (c + 1) * members]
             for s in range(slot_count):
-                parts.append(jnp.where(where == s, value, 0.0).astype(bf16))
+                parts.append(jnp.where(where == bf16(s), value, bf16(0)))
         pieces = nn(jnp.concatenate(parts, axis=0), test_fn[...]).astype(bf16)
         for side in range(2):
             shift = (1 - r if side == 0 else r) * strip
@@ -611,7 +626,8 @@
         summed = nn(onehot[side], pieces)
         return summed if first else acc[side] + summed
 
-    for k, z in enumerate(line):
+    for k, c in enumerate((0, 2, 3, 1)):
+        z = line[c]
         places = [at * lo + z for at in near]
         for at in places[1:]:
             wait_slot(at)

time: 44.3 us -> 44.3 us (level)
  no operation moved by 1% of the time
where the time goes in v5:
time: 44.3 us; the launch traced here: 44.1 us
  Pallas kernels  43.2 us (98%)
  local copies, waits for them, and re-layouts  0.97 us (2%)
    pallas_call x1, Pallas kernels, fused(): pl.pallas_call(functools.partial(fused_kernel, sizes, gy), out_shape=pltp...  43.2 us
    unnamed x1, local copies, waits for them, and re-layouts  0.97 us

profile of v5, /device:TPU:7, one launch (start us, length us, event | category | flops | bytes accessed | tf_op | source)
XLA Modules:
  0.0 44.1 jit_solution(17857041190891741975)
XLA Ops:
  0.0 43.2 %remap.1 = f32[32,16,512]{2,1,0:T(8,128)S(1)} custom-call(bf16[512,512]{1,0:T(8,128)(2,1)} %src.1, s32[32,1024]{1,0:T(8,128)} %bitcast.4, s32[4,32]{1,0:T(4,128)} %bitcast.5, s32[4,32]{1,0:T(4,128)} %bitcast.6, f32[1,32]{1,0:T(1,128)} %bitcast.7, bf16[1024,512]{1,0:T(8,128)(2,1)} %vander_hbm.1, bf16[1024,512]{1,0:T(8,128)(2,1)} %test_hbm.1, ...), custom_call_target="tpu_custom_call" | custom-call | tf_op jit(solution)/shard_map/remap/pallas_call | solution.py:793
  43.2 1.0 %copy.13 = f32[32,16,512]{2,1,0:T(8,128)} copy(f32[32,16,512]{2,1,0:T(8,128)S(1)} %remap.1) | data formatting | bytes 2097152

commit v6 on v5

--- a/solution.py
+++ b/solution.py
@@ -576,6 +576,8 @@
             device_id=core,
             device_id_type=MESH,
         ).wait_recv()
+
+    def wait_meta(at):
         pltpu.make_async_remote_copy(
             src_ref=metas.at[at],
             dst_ref=metas.at[at],
@@ -626,6 +628,9 @@
         summed = nn(onehot[side], pieces)
         return summed if first else acc[side] + summed
 
+    for k, z in enumerate(line):
+        for at_h in near[0 if k else 1 :]:
+            wait_meta(at_h * lo + z)
     for k, c in enumerate((0, 2, 3, 1)):
         z = line[c]
         places = [at * lo + z for at in near]

time: 44.3 us -> 44.3 us (level)
  no operation moved by 1% of the time
where the time goes in v6:
time: 44.3 us; the launch traced here: 44.1 us
  Pallas kernels  43.1 us (97%)
  local copies, waits for them, and re-layouts  0.97 us (2%)
    pallas_call x1, Pallas kernels, fused(): pl.pallas_call(functools.partial(fused_kernel, sizes, gy), out_shape=pltp...  43.1 us
    unnamed x1, local copies, waits for them, and re-layouts  0.97 us

profile of v6, /device:TPU:7, one launch (start us, length us, event | category | flops | bytes accessed | tf_op | source)
XLA Modules:
  0.0 44.1 jit_solution(17495448361281093735)
XLA Ops:
  0.0 43.1 %remap.1 = f32[32,16,512]{2,1,0:T(8,128)S(1)} custom-call(bf16[512,512]{1,0:T(8,128)(2,1)} %src.1, s32[32,1024]{1,0:T(8,128)} %bitcast.4, s32[4,32]{1,0:T(4,128)} %bitcast.5, s32[4,32]{1,0:T(4,128)} %bitcast.6, f32[1,32]{1,0:T(1,128)} %bitcast.7, bf16[1024,512]{1,0:T(8,128)(2,1)} %vander_hbm.1, bf16[1024,512]{1,0:T(8,128)(2,1)} %test_hbm.1, ...), custom_call_target="tpu_custom_call" | custom-call | tf_op jit(solution)/shard_map/remap/pallas_call | solution.py:798
  43.2 1.0 %copy.13 = f32[32,16,512]{2,1,0:T(8,128)} copy(f32[32,16,512]{2,1,0:T(8,128)S(1)} %remap.1) | data formatting | bytes 2097152
